TPU v7x, 256 devices: a whole 4x4x8 slice. The times are simulated.
256 devices in a mesh: hst: 32 (over z, y), local: 8 (over x, core).
Axes of the slice: x: 4, y: 4, z: 8, core: 2. Of those that a mesh axis runs over, the one named last changes fastest.
Arguments:
- embedding: float32 [524288, 256], P(('hst', 'local')), may hold values from -6 to 6
- row_accum: float32 [524288], P(('hst', 'local')), may hold values from 0.5 to 8
- lookup_grads: bfloat16 [524288, 256], P(('hst', 'local')), may hold values from -3 to 3
- lookup_slot: int32 [524288], P(('hst', 'local')), may hold values from 0 to 8191, as said below
- owner_rows: int32 [256, 32, 32], P(('hst', 'local')), may hold values from -1 to 2047, as said below
Outputs:
- new_embedding: float32 [524288, 256], P(('hst', 'local'))
- new_accum: float32 [524288], P(('hst', 'local'))
- fresh_rows: bfloat16 [524288, 256], P(('hst', 'local'))
Inputs may be any that keep to these rules, and one draw needn't show every extreme that they name: For a lookup of host s, lookup_slot = o * 32 + c with owner device o and c below that host's count of live slots for o; owners with low numbers are looked up far more often. owner_rows[o, s, c] is live (not -1) exactly for c below a count of 1 to 32; every (o, s) with o mod 32 equal to s has 32 live slots; live rows of one (o, s) are distinct; a few leading slots name the same row for every host s.
All inputs are finite; a program needn't handle non-finite values.
Results may differ from a plain program's by a relative error of at most 0.0039.
Values may be sent and summed in bfloat16 or wider, within the bound.
A program may use at most 64 MiB of HBM per device.

v0:
```python
import jax
import jax.numpy as jnp
from jax import lax
from jax.sharding import PartitionSpec as P


def local(embedding, row_accum, lookup_grads, lookup_slot, owner_rows):
    n_hst = lax.axis_size("hst")
    n_local = lax.axis_size("local")
    rows_dev, feat_width = embedding.shape
    capacity = owner_rows.shape[2]
    slot_count = n_hst * n_local * capacity
    onehot = (lookup_slot[:, None] == jnp.arange(slot_count, dtype=jnp.int32)[None, :]).astype(
        jnp.bfloat16
    )
    partial_value = lax.dot_general(
        onehot, lookup_grads, (((0,), (0,)), ((), ())), preferred_element_type=jnp.float32
    )
    partial_value = partial_value.astype(jnp.bfloat16).reshape(n_hst, n_local, capacity, feat_width)
    moved = lax.all_to_all(partial_value, "hst", split_axis=0, concat_axis=0, tiled=True)
    received = (
        lax.psum_scatter(moved, "local", scatter_dimension=1, tiled=True)
        .astype(jnp.float32)
        .astype(jnp.bfloat16)
    )
    received = received.astype(jnp.float32)
    row_ids = owner_rows.reshape(n_hst * capacity)
    is_live = row_ids >= 0
    target = jnp.where(is_live, row_ids, rows_dev)
    row_grad = jax.ops.segment_sum(
        received.reshape(n_hst * capacity, feat_width), target, num_segments=rows_dev + 1
    )[:rows_dev]
    new_accum = row_accum + jnp.mean(row_grad * row_grad, axis=1)
    new_embedding = embedding - 0.1 * row_grad / jnp.sqrt(new_accum)[:, None]
    safe_rows = jnp.where(is_live, row_ids, 0)
    picked = jnp.take(new_embedding, safe_rows, axis=0)
    picked = jnp.where(is_live[:, None], picked, 0.0).astype(jnp.bfloat16)
    picked = picked.reshape(n_hst, 1, capacity, feat_width)
    returned = lax.all_to_all(picked, "hst", split_axis=0, concat_axis=0, tiled=True)
    host_cache = lax.all_gather(returned, "local", axis=1, tiled=True).reshape(
        slot_count, feat_width
    )
    fresh_rows = jnp.take(host_cache, lookup_slot, axis=0)
    return (new_embedding, new_accum, fresh_rows)


def solution(mesh):
    return jax.shard_map(
        local,
        mesh=mesh,
        in_specs=(
            P(("hst", "local"), None),
            P(("hst", "local")),
            P(("hst", "local"), None),
            P(("hst", "local")),
            P(("hst", "local"), None, None),
        ),
        out_specs=(P(("hst", "local"), None), P(("hst", "local")), P(("hst", "local"), None)),
        check_vma=False,
    )
```

profile of v0, /device:TPU:1, one launch (start us, length us, event | category | flops | bytes accessed | tf_op | source)
XLA Modules:
  0.0 310.2 jit_solution(12631022377669129002)
XLA Ops:
  7.2 0.0 copy-start
  7.2 0.0 all-reduce.3.cloned.1.call-start
  7.2 1.2 copy-done
  8.4 20.3 %fusion.2 = bf16[8192,256]{1,0:T(8,128)(2,1)S(1)} fusion(bf16[2048,256]{1,0:T(8,128)(2,1)S(1)} %copy-done, s32[2048]{0:T(1024)} %param.8), kind=kOutput, calls=%fused_computation.6 | convolution fusion | flops 8608808960 | bytes 5251072 | tf_op jit(solution)/shard_map/dot_general | solution.py:16
  28.7 105.6 %all_to_all.10 = bf16[32,8,32,256]{3,2,1,0:T(8,128)(2,1)} all-to-all(bf16[32,8,32,256]{3,2,1,0:T(8,128)(2,1)S(1)} %bitcast.28), channel_id=1, replica_groups=mesh['hst'=32,'local'=8] {'hst'}, dimensions={0} | all-to-all | bytes 8388608 | tf_op jit(solution)/shard_map/all_to_all | solution.py:20
  134.3 0.0 copy-start.4
  134.3 0.0 copy-start.7
  134.3 0.0 all-reduce.3.cloned.1.call-update
  134.3 0.0 all-gather.2.cloned.1.call-start
  134.4 0.6 copy-done.4
  135.0 0.1 reshape.111
  135.1 0.0 copy-done.7
  135.1 0.6 dynamic-slice
  135.7 73.9 %all-reduce.3.cloned.1.call-done = bf16[32,8,32,256]{3,2,1,0:T(8,128)(2,1)} async-done(((bf16[32,8,32,256]{3,2,1,0:T(8,128)(2,1)}), bf16[32,8,32,256]{3,2,1,0:T(8,128)(2,1)}) %all-reduce.3.cloned.1.call-update) | async-done | bytes 4194320
  209.6 2.5 constant_dynamic-slice_fusion
  212.2 0.0 copy-start.6
  212.2 6.9 %scatter_custom_fusion = f32[2049,256]{1,0:T(8,128)S(1)} fusion(s32[1024]{0:T(1024)S(1)} %bitcast.33, f32[]{:T(128)} %constant.19.clone.1, bf16[1024,256]{1,0:T(8,128)(2,1)} %bitcast.30), kind=kCustom, calls=%fused_computation.9 | custom fusion | flops 524288 | bytes 2622468 | tf_op jit(solution)/shard_map/scatter-add | solution.py:30
  219.0 0.0 copy-start.2
  219.0 0.0 copy-start.3
  219.0 0.3 multiply_reduce_fusion
  219.4 0.0 copy-done.6
  219.4 0.6 fusion.7
  220.0 0.4 copy-done.2
  220.4 1.0 copy-done.3
  221.4 2.0 divide_subtract_fusion
  223.4 0.0 copy-start.1
  223.4 4.6 %gather_fusion = bf16[1024,256]{1,0:T(8,128)(2,1)} fusion(f32[2048,256]{1,0:T(8,128)S(1)} %divide_subtract_fusion, s32[1024]{0:T(1024)S(1)} %broadcast_clamp_fusion), kind=kCustom, calls=%fused_computation | custom fusion | bytes 1052672 | tf_op jit(solution)/shard_map/jit(_take)/gather | solution.py:36
  228.0 0.0 copy-done.1
  228.0 0.0 copy-start.5
  228.0 1.4 select_convert_fusion
  229.4 23.9 %all_to_all.11 = bf16[32,1,32,256]{3,2,1,0:T(8,128)(2,1)} all-to-all(bf16[32,1,32,256]{3,2,1,0:T(8,128)(2,1)S(1)} %select_convert_fusion), channel_id=1, replica_groups=mesh['hst'=32,'local'=8] {'hst'}, dimensions={0} | all-to-all | bytes 1048576 | tf_op jit(solution)/shard_map/all_to_all | solution.py:39
  253.2 0.0 all-gather.2.cloned.1.call-update
  253.3 0.0 copy-done.5
  253.3 34.7 %all-gather.2.cloned.1.call-done = bf16[32,8,32,256]{3,2,0,1:T(8,128)(2,1)} async-done(((bf16[32,1,32,256]{3,2,0,1:T(8,128)(2,1)}), bf16[32,8,32,256]{3,2,0,1:T(8,128)(2,1)}) %all-gather.2.cloned.1.call-update) | async-done | bytes 4194320 | tf_op jit(solution)/shard_map/all_gather | solution.py:40
  288.0 4.8 %copy.11 = bf16[32,8,32,256]{3,2,1,0:T(8,128)(2,1)} copy(bf16[32,8,32,256]{3,2,0,1:T(8,128)(2,1)} %all-gather.2.cloned.1.call-done) | data formatting | bytes 8388608 | tf_op jit(solution)/shard_map/all_gather | solution.py:40
  292.8 9.4 %gather_fusion.1 = bf16[2048,256]{1,0:T(8,128)(2,1)S(1)} fusion(bf16[8192,256]{1,0:T(8,128)(2,1)} %bitcast.27, s32[2048]{0:T(1024)S(1)} %fusion.6), kind=kCustom, calls=%fused_computation.1 | custom fusion | bytes 2105344 | tf_op jit(solution)/shard_map/jit(_take)/gather | solution.py:43
  302.2 1.2 broadcast_select_fusion
  (5 shorter events, 0.0 us)
Async XLA Ops:
  7.2 1.2 copy-start
  7.2 202.5 %all-reduce.3.cloned.1.call-start = ((), (), s32[]{:S(2)}) async-start(), calls=%async_computation.3 | async-start | bytes 8388608
  134.3 0.7 copy-start.4
  134.3 0.8 copy-start.7
  134.3 153.7 %all-gather.2.cloned.1.call-start = ((), (), s32[]{:S(2)}) async-start(), calls=%async_computation.2 | async-start | bytes 4718592 | tf_op jit(solution)/shard_map/all_gather | solution.py:40
  212.2 7.2 %copy-start.6 = (f32[2048]{0:T(1024)S(1)}, f32[2048]{0:T(1024)}, u32[]{:S(2)}) copy-start(f32[2048]{0:T(1024)} %param.6) | copy-start | bytes 24580
  219.0 1.3 copy-start.2
  219.0 2.4 copy-start.3
  223.4 4.6 %copy-start.1 = (f32[2048,256]{1,0:T(8,128)}, f32[2048,256]{1,0:T(8,128)S(1)}, u32[]{:S(2)}) copy-start(f32[2048,256]{1,0:T(8,128)S(1)} %divide_subtract_fusion) | copy-start | bytes 6291460
  228.0 25.3 %copy-start.5 = (s32[2048]{0:T(1024)S(1)}, s32[2048]{0:T(1024)}, u32[]{:S(2)}) copy-start(s32[2048]{0:T(1024)} %param.8) | copy-start | bytes 24580
Sparse Core Ops, SparseCore 0:
  134.4 75.1 all-reduce.2
  253.4 34.5 all-gather.1
where the time goes:
time: 311 us; the launch traced here: 310 us
  blocking collectives  129 us (41%)
  waiting for transfers between devices  109 us (35%)
  local copies, waits for them, and re-layouts  25.2 us (8%)
  matrix products  20.3 us (7%)
  between operations  14.2 us (5%)
  other arithmetic  12.4 us (4%)
    all_to_all x1, blocking collectives, local(): lax.all_to_all(partial_value, 'hst', split_axis=0, concat_axis=0, tiled=T...  106 us
    unnamed x3, waiting for transfers between devices  74 us
    all_gather x1, waiting for transfers between devices, local(): lax.all_gather(returned, 'local', axis=1, tiled=True)  34.7 us
    all_to_all x1, blocking collectives, local(): lax.all_to_all(picked, 'hst', split_axis=0, concat_axis=0, tiled=True)  23.9 us
    dot_general x1, matrix products, local(): lax.dot_general(onehot, lookup_grads, (((0,), (0,)), ((), ())), preferred...  20.3 us
    gather x1, local copies, waits for them, and re-layouts, local(): fresh_rows = jnp.take(host_cache, lookup_slot, axis=0)  9.36 us
    scatter-add x1, other arithmetic, local(): jax.ops.segment_sum(received.reshape(n_hst * capacity, feat_width), targe...  6.86 us
    unnamed x18, local copies, waits for them, and re-layouts  6.32 us
  transfers between devices with their start and end apart: 2, of which 2 were waited for; matrix products, arithmetic and copies ran while one was open for 0% of the time, Pallas kernels for 0%

commit v1 on v0

v1 whole, which is shorter than its diff:
```python
import functools

import jax
import jax.numpy as jnp
from jax import lax
from jax.experimental import pallas as pl
from jax.experimental.pallas import tpu as pltpu
from jax.sharding import PartitionSpec as P

MESH = pl.DeviceIdType.MESH
F32 = jnp.float32
BF16 = jnp.bfloat16
NY = 4
LANES = 128


def plane_dz(plane, nz):
    group, half = divmod(plane, 2)
    if half == 0:
        return nz // 2 - group
    return (nz // 2 + group) % nz if group else 0


def plane_of(dz, nz):
    return next(p for p in range(nz) if plane_dz(p, nz) == dz % nz)


def kernel(
    nz, ny, cap,
    slot_ref, g_hbm, orow_ref, accum_ref, emb_hbm,
    newemb_hbm, newacc_ref, fresh_ref,
    slots, g_all, fkey, facc, fsend, frecv, fin, grecv, rg, emb_v, embbf, pick, cache, ekey, gacc,
    load_sem, d2d_send, d2d_recv, fs_sem, fr_sem, as_sem, ar_sem, rs_sem, rr_sem, gs_sem, gr_sem, out_sem,
):
    n_hst = nz * ny
    tokens, feat = g_hbm.shape
    rows = emb_hbm.shape[0]
    nt = tokens // LANES
    n_groups = nz // 2
    plane_rows = ny * cap

    h = lax.axis_index("hst")
    l = lax.axis_index("local")
    z, y = h // ny, h % ny
    x, core = l // 2, l % 2
    right = lax.rem(x + 1, 4) * 2 + core
    left = lax.rem(x + 3, 4) * 2 + core
    sib = x * 2 + 1 - core

    barrier = pltpu.get_barrier_semaphore()

    def greet(d, carry):
        peer = lax.rem(h + d, n_hst)
        pl.semaphore_signal(barrier, inc=1, device_id=(peer, l), device_id_type=MESH)
        return carry

    for peer in (sib, right, left):
        pl.semaphore_signal(barrier, inc=1, device_id=(h, peer), device_id_type=MESH)
    lax.fori_loop(1, n_hst, greet, 0)

    load_g = pltpu.make_async_copy(g_hbm, g_all.at[0], load_sem.at[0])
    load_g.start()
    load_e = pltpu.make_async_copy(emb_hbm, emb_v, load_sem.at[1])
    load_e.start()

    def remote(src, dst, ssem, rsem, hh, ll):
        return pltpu.make_async_remote_copy(
            src_ref=src, dst_ref=dst, send_sem=ssem, recv_sem=rsem, device_id=(hh, ll), device_id_type=MESH
        )

    def decode(s):
        position = s % cap
        owner = s // cap
        ol = owner % 8
        oh = owner // 8
        lo = (oh % ny) * cap + position
        dz = (oh // ny - z + nz) % nz
        half = jnp.where((dz >= 1) & (dz <= nz // 2), 0, 1)
        group = jnp.where(half == 0, nz // 2 - dz, jnp.where(dz == 0, 0, dz - nz // 2))
        dx = (ol // 2 - x + 4) % 4
        dcore = (ol % 2 - core + 2) % 2
        return lo, group, half, dx, dcore

    def forward_key(s):
        lo, group, half, dx, dcore = decode(s)
        return jnp.where(dcore == 0, (group * 8 + dx * 2 + half) * LANES + lo, -4096).astype(F32)

    own_slots = slot_ref[...]
    fkey[0] = forward_key(own_slots)

    pl.semaphore_wait(barrier, n_hst - 1 + 3)

    d2d = [
        remote(slot_ref, slots, d2d_send.at[0], d2d_recv.at[0], h, sib),
        remote(g_hbm, g_all.at[1], d2d_send.at[1], d2d_recv.at[1], h, sib),
    ]
    for c in d2d:
        c.start()

    sub_iota = lax.broadcasted_iota(jnp.int32, (LANES, LANES), 0)
    lane_iota = lax.broadcasted_iota(jnp.int32, (LANES, LANES), 1)
    sub_bf = sub_iota.astype(F32).astype(BF16)
    one = jnp.ones((LANES, LANES), BF16)
    zero = jnp.zeros((LANES, LANES), BF16)

    def row_hot(key_row, base):
        rel = jnp.broadcast_to(key_row - base, (LANES, LANES)).astype(BF16)
        return jnp.where(rel == sub_bf, one, zero)

    kt = min(512, tokens)
    per_tile = kt // LANES

    def forward_part(group, core_index):
        def step(k, carry):
            hot = []
            for b in range(8):
                base = float((group * 8 + b) * LANES)
                hot.append(
                    jnp.concatenate(
                        [row_hot(fkey[core_index, pl.ds(k * per_tile + i, 1), :], base) for i in range(per_tile)], axis=1
                    )
                )
            hot = jnp.concatenate(hot, axis=0)
            part = jnp.dot(
                hot, g_all[core_index, pl.ds(pl.multiple_of(k * kt, kt), kt), :], preferred_element_type=F32
            )
            facc[group] += part.reshape(8, plane_rows, feat)
            return carry

        lax.fori_loop(0, tokens // kt, step, 0)

    block_of = (4, 5, 3, 6, 2, 7)

    def forward_send(group, index, value):
        fsend[group, index] = value.astype(BF16)
        c = remote(
            fsend.at[group, index], frecv.at[group, index], fs_sem.at[group, index], fr_sem.at[group, index],
            h, right if index in (0, 2, 4) else left,
        )
        c.start()
        return c

    sends = []

    def fwait(group, index):
        remote(
            fsend.at[group, index], frecv.at[group, index], fs_sem.at[group, index], fr_sem.at[group, index], h, right
        ).wait_recv()

    def merge(group):
        for index, far in ((4, 0), (5, 1)):
            fwait(group, far)
            sends.append(
                forward_send(group, index, facc[group, block_of[index]] + frecv[group, far].astype(F32))
            )

    def scatter_hosts(src_plane, dst_plane, ssem, rsem, dz):
        for dy in range(ny):
            if dz == 0 and dy == 0:
                continue
            py = lax.rem(y + dy, ny)
            peer = lax.rem(z + dz, nz) * ny + py
            remote(src_plane.at[py], dst_plane.at[y], ssem, rsem, peer, l).start()

    def wait_hosts(src_plane, dst_plane, ssem, rsem, dz, what):
        count = ny - 1 if dz == 0 else ny
        c = remote(src_plane.at[pl.ds(0, count)], dst_plane.at[pl.ds(0, count)], ssem, rsem, h, sib)
        c.wait_send() if what == "send" else c.wait_recv()

    def finalize(group):
        for half, (from_left, from_right) in enumerate(((4, 3), (2, 5))):
            plane = 2 * group + half
            dz = plane_dz(plane, nz)
            back = plane_of(-dz, nz)
            fwait(group, from_left)
            fwait(group, from_right)
            total = facc[group, half] + frecv[group, from_left].astype(F32) + frecv[group, from_right].astype(F32)
            fin[plane] = total.astype(BF16).reshape(ny, cap, feat)
            scatter_hosts(fin.at[plane], grecv.at[back], as_sem.at[plane], ar_sem.at[back], dz)
            if dz == 0:
                grecv[plane, y] = fin[plane, y]

    rg[...] = jnp.zeros_like(rg)

    def owner_row(plane):
        return orow_ref[pl.ds(lax.rem(z + plane_dz(plane, nz), nz), 1), :].astype(F32)

    def accumulate(group):
        planes = (2 * group, 2 * group + 1)
        for plane in planes:
            wait_hosts(fin.at[plane], grecv.at[plane], as_sem.at[plane], ar_sem.at[plane], plane_dz(plane, nz), "recv")
        data = grecv[pl.ds(2 * group, 2)].reshape(2 * plane_rows, feat)
        keys = [owner_row(plane) for plane in planes]
        span = min(512, rows)

        def step(r, carry):
            start = pl.multiple_of(r * span, span)
            base = (r * span).astype(F32)
            hot = jnp.concatenate(
                [
                    jnp.concatenate([row_hot(key, base + float(i * LANES)) for key in keys], axis=1)
                    for i in range(span // LANES)
                ],
                axis=0,
            )
            rg[pl.ds(start, span), :] += jnp.dot(hot, data, preferred_element_type=F32)
            return carry

        lax.fori_loop(0, rows // span, step, 0)

    load_g.wait()
    for group in range(n_groups):
        facc[group] = jnp.zeros((8, plane_rows, feat), F32)
        forward_part(group, 0)
        if group == 0:
            for c in d2d:
                c.wait()
            fkey[1] = forward_key(slots[...])
        forward_part(group, 1)
        for index in (0, 1, 2, 3):
            sends.append(forward_send(group, index, facc[group, block_of[index]]))
        if group >= 1:
            merge(group - 1)
        if group >= 2:
            finalize(group - 2)
    if n_groups >= 2:
        finalize(n_groups - 2)
    merge(n_groups - 1)

    def column(row):
        return jnp.broadcast_to(row.astype(F32), (LANES, LANES)).T.astype(jnp.int32)

    def column_key(hi, lo):
        return jnp.where(lane_iota == column(lo), column(hi), -1).astype(F32).astype(BF16)

    lo, group_, half_, dx, dcore = decode(own_slots)
    hi = (dx * 2 + dcore) * nz + group_ * 2 + half_
    for i in range(nt):
        ekey[pl.ds(i * LANES, LANES), :] = column_key(hi[i : i + 1, :], lo[i : i + 1, :])
    load_e.wait()
    gacc[...] = jnp.zeros_like(gacc)

    for group in range(max(n_groups - 2, 0)):
        accumulate(group)
    finalize(n_groups - 1)
    for group in range(max(n_groups - 2, 0), n_groups):
        accumulate(group)

    eye = sub_iota == lane_iota

    def update(i, carry):
        start = pl.multiple_of(i * LANES, LANES)
        grad = rg[pl.ds(start, LANES), :]
        mean = jnp.sum(grad * grad, axis=1, keepdims=True) * (1.0 / feat)
        old = jnp.broadcast_to(accum_ref[pl.ds(i, 1), :], (LANES, LANES)).T
        new = old + mean
        newacc_ref[pl.ds(i, 1), :] = jnp.sum(jnp.where(eye, new, 0.0), axis=0, keepdims=True)
        scale = 0.1 / jnp.sqrt(new)
        scale = jnp.concatenate([scale] * (feat // LANES), axis=1)
        fresh = emb_v[pl.ds(start, LANES), :] - grad * scale
        emb_v[pl.ds(start, LANES), :] = fresh
        embbf[pl.ds(start, LANES), :] = fresh.astype(BF16)
        return carry

    lax.fori_loop(0, rows // LANES, update, 0)
    store_e = pltpu.make_async_copy(emb_v, newemb_hbm, out_sem.at[0])
    store_e.start()

    one_c = jnp.ones((2 * plane_rows, LANES), BF16)
    zero_c = jnp.zeros((2 * plane_rows, LANES), BF16)

    def send_back(group):
        key = jnp.concatenate(
            [
                column_key(jnp.floor(owner_row(p) * (1.0 / LANES)), owner_row(p) - LANES * jnp.floor(owner_row(p) * (1.0 / LANES)))
                for p in (2 * group, 2 * group + 1)
            ],
            axis=0,
        )
        hot = jnp.concatenate(
            [jnp.where(key == jnp.asarray(b, BF16), one_c, zero_c) for b in range(rows // LANES)], axis=1
        )
        got = jnp.dot(hot, embbf[...], preferred_element_type=F32).astype(BF16)
        for half in range(2):
            plane = 2 * group + half
            dz = plane_dz(plane, nz)
            back = plane_of(-dz, nz)
            pick[plane] = got[half * plane_rows : (half + 1) * plane_rows].reshape(ny, cap, feat)
            scatter_hosts(pick.at[plane], cache.at[0, back], rs_sem.at[plane], rr_sem.at[back], dz)
            if dz == 0:
                cache[0, plane, y] = pick[plane, y]

    def gather_copy(group, index):
        pair, first, second = pl.ds(2 * group, 2), 2 * group, 2 * group + 1
        src, dst, to = (
            (cache.at[0, pair], cache.at[6, pair], right),
            (cache.at[0, pair], cache.at[2, pair], left),
            (cache.at[0, pair], cache.at[1, pair], sib),
            (cache.at[6, pair], cache.at[7, pair], sib),
            (cache.at[6, first], cache.at[4, first], right),
            (cache.at[2, pair], cache.at[3, pair], sib),
            (cache.at[2, second], cache.at[4, second], left),
            (cache.at[4, first], cache.at[5, first], sib),
            (cache.at[4, second], cache.at[5, second], sib),
        )[index]
        return remote(src, dst, gs_sem.at[group, index], gr_sem.at[group, index], h, to)

    def own_arrived(group):
        for plane in (2 * group, 2 * group + 1):
            wait_hosts(
                pick.at[plane], cache.at[0, plane], rs_sem.at[plane], rr_sem.at[plane], plane_dz(plane, nz), "recv"
            )
        for index in (0, 1, 2):
            gather_copy(group, index).start()

    def near_arrived(group):
        gather_copy(group, 0).wait_recv()
        gather_copy(group, 4).start()
        gather_copy(group, 3).start()
        gather_copy(group, 1).wait_recv()
        gather_copy(group, 6).start()
        gather_copy(group, 5).start()

    def far_arrived(group):
        gather_copy(group, 4).wait_recv()
        gather_copy(group, 7).start()
        gather_copy(group, 6).wait_recv()
        gather_copy(group, 8).start()

    tt = min(512, tokens)
    one_g = jnp.ones((tt, LANES), BF16)
    zero_g = jnp.zeros((tt, LANES), BF16)

    def look_up(chunks, last=False):
        for lane, group in chunks:
            for index in {1: (2,), 7: (3,), 3: (5,), 5: (7, 8)}.get(lane, ()):
                gather_copy(group, index).wait_recv()

        def step(i, carry):
            span = pl.ds(pl.multiple_of(i * tt, tt), tt)
            key = ekey[span, :]
            total = gacc[span, :]
            for lane, group in chunks:
                first = lane * nz + 2 * group
                hot = jnp.concatenate(
                    [jnp.where(key == jnp.asarray(b, BF16), one_g, zero_g) for b in (first, first + 1)], axis=1
                )
                data = cache[lane, pl.ds(2 * group, 2)].reshape(2 * plane_rows, feat)
                total += jnp.dot(hot, data, preferred_element_type=F32)
            if last:
                fresh_ref[span, :] = total.astype(BF16)
            else:
                gacc[span, :] = total
            return carry

        lax.fori_loop(0, tokens // tt, step, 0)

    order = list(range(n_groups - 1, -1, -1))
    for group in order:
        send_back(group)
    for i, group in enumerate(order):
        own_arrived(group)
        if i >= 1:
            near_arrived(order[i - 1])
            look_up([(0, group), (1, order[i - 1])])
        else:
            look_up([(0, group)])
        if i >= 2:
            far_arrived(order[i - 2])
            look_up([(6, order[i - 2]), (2, order[i - 2]), (7, order[i - 2]), (3, order[i - 2])])
        if i >= 3:
            look_up([(4, order[i - 3]), (5, order[i - 3])])
    near_arrived(order[-1])
    look_up([(1, order[-1])])
    if n_groups >= 2:
        far_arrived(order[-2])
        look_up([(6, order[-2]), (2, order[-2]), (7, order[-2]), (3, order[-2])])
    if n_groups >= 3:
        look_up([(4, order[-3]), (5, order[-3])])
    look_up([(6, order[-1]), (2, order[-1]), (7, order[-1]), (3, order[-1])])
    far_arrived(order[-1])
    if n_groups >= 2:
        look_up([(4, order[-2]), (5, order[-2])])
    look_up([(4, order[-1]), (5, order[-1])], last=True)

    store_e.wait()
    for c in sends:
        c.wait_send()
    for plane in range(nz):
        dz = plane_dz(plane, nz)
        wait_hosts(fin.at[plane], grecv.at[plane], as_sem.at[plane], ar_sem.at[plane], dz, "send")
        wait_hosts(pick.at[plane], cache.at[0, plane], rs_sem.at[plane], rr_sem.at[plane], dz, "send")
    for group in range(n_groups):
        for index in range(9):
            gather_copy(group, index).wait_send()


def local(ny, embedding, row_accum, lookup_grads, lookup_slot, owner_rows):
    n_hst = lax.axis_size("hst")
    nz = n_hst // ny
    rows, feat = embedding.shape
    tokens = lookup_slot.shape[0]
    cap = owner_rows.shape[2]
    nt = tokens // LANES
    groups = nz // 2
    plane = ny * cap
    vmem = pl.BlockSpec(memory_space=pltpu.VMEM)
    hbm = pl.BlockSpec(memory_space=pl.ANY)
    dma = pltpu.SemaphoreType.DMA
    new_embedding, new_accum, fresh = pl.pallas_call(
        functools.partial(kernel, nz, ny, cap),
        out_shape=(
            jax.ShapeDtypeStruct((rows, feat), F32),
            jax.ShapeDtypeStruct((rows // LANES, LANES), F32),
            jax.ShapeDtypeStruct((tokens, feat), BF16),
        ),
        in_specs=[vmem, hbm, vmem, vmem, hbm],
        out_specs=(hbm, vmem, vmem),
        scratch_shapes=[
            pltpu.VMEM((nt, LANES), jnp.int32),
            pltpu.VMEM((2, tokens, feat), BF16),
            pltpu.VMEM((2, nt, LANES), F32),
            pltpu.VMEM((groups, 8, plane, feat), F32),
            pltpu.VMEM((groups, 6, plane, feat), BF16),
            pltpu.VMEM((groups, 6, plane, feat), BF16),
            pltpu.VMEM((nz, ny, cap, feat), BF16),
            pltpu.VMEM((nz, ny, cap, feat), BF16),
            pltpu.VMEM((rows, feat), F32),
            pltpu.VMEM((rows, feat), F32),
            pltpu.VMEM((rows, feat), BF16),
            pltpu.VMEM((nz, ny, cap, feat), BF16),
            pltpu.VMEM((8, nz, ny, cap, feat), BF16),
            pltpu.VMEM((tokens, LANES), BF16),
            pltpu.VMEM((tokens, feat), F32),
            dma((2,)),
            dma((2,)),
            dma((2,)),
            dma((groups, 6)),
            dma((groups, 6)),
            dma((nz,)),
            dma((nz,)),
            dma((nz,)),
            dma((nz,)),
            dma((groups, 9)),
            dma((groups, 9)),
            dma((1,)),
        ],
        compiler_params=pltpu.CompilerParams(
            collective_id=0, has_side_effects=True, vmem_limit_bytes=56 * 1024 * 1024
        ),
    )(
        lookup_slot.reshape(nt, LANES),
        lookup_grads,
        owner_rows.reshape(nz, plane),
        row_accum.reshape(rows // LANES, LANES),
        embedding,
    )
    return new_embedding, new_accum.reshape(rows), fresh


def solution(mesh, ny=NY):
    both = ("hst", "local")
    return jax.shard_map(
        functools.partial(local, ny),
        mesh=mesh,
        in_specs=(P(both, None), P(both), P(both, None), P(both), P(both, None, None)),
        out_specs=(P(both, None), P(both), P(both, None)),
        check_vma=False,
    )
```

time: 311 us -> 92.5 us (0.30)
  blocking collectives: 129 us -> 0 us
  waiting for transfers between devices: 109 us -> 0 us
  Pallas kernels: 0 us -> 85.5 us
  matrix products: 20.3 us -> 0 us
  local copies, waits for them, and re-layouts: 25.2 us -> 6.09 us
  between operations: 14.2 us -> 0.66 us
  other arithmetic: 12.4 us -> 0 us
    all_to_all x2 -> x0, blocking collectives: 129 us -> none  [the longest x1 106 us: local(): lax.all_to_all(partial_value, 'hst', split_axis=0, concat_axis=0, tiled=T...]
    pallas_call x0 -> x1, Pallas kernels: none -> 85.5 us  [local(): pl.pallas_call(functools.partial(kernel, nz, ny, cap), out_shape=(jax.Sha...]
    unnamed x3 -> x0, waiting for transfers between devices: 74 us -> none
    all_gather x1 -> x0, waiting for transfers between devices: 34.7 us -> none  [local(): lax.all_gather(returned, 'local', axis=1, tiled=True)]
    dot_general x1 -> x0, matrix products: 20.3 us -> none  [local(): lax.dot_general(onehot, lookup_grads, (((0,), (0,)), ((), ())), preferred...]
    gather x2 -> x0, local copies, waits for them, and re-layouts: 14 us -> none  [the longest x1 9.36 us: local(): fresh_rows = jnp.take(host_cache, lookup_slot, axis=0)]
    scatter-add x1 -> x0, other arithmetic: 6.86 us -> none  [local(): jax.ops.segment_sum(received.reshape(n_hst * capacity, feat_width), targe...]
    all_gather x1 -> x0, local copies, waits for them, and re-layouts: 4.81 us -> none  [local(): lax.all_gather(returned, 'local', axis=1, tiled=True)]
  transfers between devices with their start and end apart: 2 -> 0, of which waited for: 2 -> 0; matrix products, arithmetic and copies ran while one was open for 0% -> 0% of each run, Pallas kernels for 0% -> 0%
where the time goes in v1:
time: 92.5 us; the launch traced here: 92.2 us
  Pallas kernels  85.5 us (92%)
  local copies, waits for them, and re-layouts  6.09 us (7%)
    pallas_call x1, Pallas kernels, local(): pl.pallas_call(functools.partial(kernel, nz, ny, cap), out_shape=(jax.Sha...  85.5 us
    unnamed x7, local copies, waits for them, and re-layouts  4.71 us

profile of v1, /device:TPU:1, one launch (start us, length us, event | category | flops | bytes accessed | tf_op | source)
XLA Modules:
  0.0 92.2 jit_solution(4647405381720224728)
XLA Ops:
  0.6 1.4 %reshape.19.orow_ref = s32[8,128]{1,0:T(8,128)} reshape(s32[1,32,32]{2,1,0:T(8,128)} %param.9) | data formatting | bytes 8192 | tf_op jit(solution)/shard_map/reshape | solution.py:454
  2.0 85.5 %shard_map.76 = (f32[2048,256]{1,0:T(8,128)}, f32[16,128]{1,0:T(8,128)}, bf16[2048,256]{1,0:T(8,128)(2,1)}) custom-call(s32[16,128]{1,0:T(8,128)} %bitcast.3, bf16[2048,256]{1,0:T(8,128)(2,1)} %g_hbm.1, s32[8,128]{1,0:T(8,128)} %reshape.19.orow_ref, f32[16,128]{1,0:T(8,128)} %bitcast.4, f32[2048,256]{1,0:T(8,128)} %emb_hbm.1), custom_call_target="tpu_custom_call" | custom-call | tf_op jit(solution)/shard_map/pallas_call | solution.py:410
  87.5 0.0 copy-start.1
  87.5 0.0 copy-start
  87.5 3.1 %copy.11 = f32[2048,256]{1,0:T(8,128)} copy(f32[2048,256]{1,0:T(8,128)} %get-tuple-element.12) | data formatting | bytes 4194304
  90.7 0.0 copy-done.1
  90.7 0.6 copy.12
  91.3 0.0 copy-done
  91.3 1.0 %copy.13 = bf16[2048,256]{1,0:T(8,128)(2,1)} copy(bf16[2048,256]{1,0:T(8,128)(2,1)S(1)} %copy-done) | data formatting | bytes 2097152
Async XLA Ops:
  87.5 3.2 %copy-start.1 = (f32[16,128]{1,0:T(8,128)S(1)}, f32[16,128]{1,0:T(8,128)}, u32[]{:S(2)}) copy-start(f32[16,128]{1,0:T(8,128)} %get-tuple-element.7) | copy-start | bytes 24580
  87.5 3.7 %copy-start = (bf16[2048,256]{1,0:T(8,128)(2,1)S(1)}, bf16[2048,256]{1,0:T(8,128)(2,1)}, u32[]{:S(2)}) copy-start(bf16[2048,256]{1,0:T(8,128)(2,1)} %get-tuple-element.14) | copy-start | bytes 3145732

commit v2 on v0

v2 whole, which is shorter than its diff:
```python
import functools

import jax
import jax.numpy as jnp
from jax import lax
from jax.experimental import pallas as pl
from jax.experimental.pallas import tpu as pltpu
from jax.sharding import PartitionSpec as P

MESH = pl.DeviceIdType.MESH
F32 = jnp.float32
BF16 = jnp.bfloat16
NY = 4
LANES = 128
SCHEDULES = {
    4: (
        "C0", "c0", "S0", "C1", "c1", "S1", "M0", "C2", "M1", "c2", "S2", "C3", "c3", "Z0", "P", "Z1", "S3", "M2", "M3",
        "Z2", "Z3", "U0", "U1", "o1", "o0", "n1", "n0", "o3", "o2", "L00,01,10,11", "f1", "f0", "L61,21,71,31", "n3",
        "n2", "L60,20,70,30", "f3", "L40,41,50,51", "L02,03,12,13", "f2", "L63,23,73,33", "L62,22,72,32,43,53", "L42,52",
    ),
    2: (
        "C0", "c0", "S0", "M0", "C1", "c1", "S1", "M1", "Z0", "Z1", "P", "U0", "U1", "o0", "n0", "L00,10", "f0",
        "L60,20,70,30", "L40,50", "o1", "n1", "L01,11", "f1", "L61,21,71,31", "L41,51",
    ),
}


def kernel(
    schedule, nz, ny, cap,
    slot_hbm, g_hbm, owner_hbm, accum_hbm, emb_hbm,
    newemb_v, acc_v, fresh_v,
    slots, owner_ref, accum_ref, g_all, fkey, orow, facc, fsend, frecv, fin, grecv, emb_v, embbf, pick, cache, ekey, gacc,
    load_sem, d2d_send, d2d_recv, fs_sem, fr_sem, as_sem, ar_sem, rs_sem, rr_sem, gs_sem, gr_sem,
):
    tokens, feat = g_hbm.shape
    rows = emb_hbm.shape[0]
    nt = tokens // LANES
    n_groups = nz // 2
    n_sub = n_groups // 2
    plane_rows = ny * cap

    h = lax.axis_index("hst")
    l = lax.axis_index("local")
    z, y = h // ny, h % ny
    x, core = l // 2, l % 2
    parity = z % 2
    right = lax.rem(x + 1, 4) * 2 + core
    left = lax.rem(x + 3, 4) * 2 + core
    sib = x * 2 + 1 - core

    barrier = pltpu.get_barrier_semaphore()

    def greet(sem, hh, ll):
        pl.semaphore_signal(sem, inc=1, device_id=(hh, ll), device_id_type=MESH)

    load_s, load_g, load_o, load_a, load_e = [
        pltpu.make_async_copy(src, dst, load_sem.at[i])
        for i, (src, dst) in enumerate(
            (
                (slot_hbm, slots.at[0]),
                (g_hbm, g_all.at[0]),
                (owner_hbm, owner_ref),
                (accum_hbm, accum_ref),
                (emb_hbm, emb_v),
            )
        )
    ]
    for c in (load_s, load_g, load_o, load_a, load_e):
        c.start()

    for peer in (sib, right, left):
        greet(barrier, h, peer)
    for d in range(1, nz * ny):
        greet(barrier, lax.rem(h + d, nz * ny), l)

    def remote(src, dst, ssem, rsem, hh, ll):
        return pltpu.make_async_remote_copy(
            src_ref=src, dst_ref=dst, send_sem=ssem, recv_sem=rsem, device_id=(hh, ll), device_id_type=MESH
        )

    def far_dz(m):
        return nz // 2 - m

    def near_dz(m):
        return jnp.where(m == 0, 0, lax.rem(nz // 2 + m, nz))

    def distance(i):
        return 2 * (i % n_sub) + lax.rem(i // n_sub + parity, 2)

    def plane_z(i, half):
        m = distance(i)
        return lax.rem(z + (near_dz(m) if half else far_dz(m)), nz)

    def decode(s):
        position = s % cap
        owner = s // cap
        ol = owner % 8
        oh = owner // 8
        lo = (oh % ny) * cap + position
        dz = (oh // ny - z + nz) % nz
        half = jnp.where((dz >= 1) & (dz <= nz // 2), 0, 1)
        m = jnp.where(half == 0, nz // 2 - dz, jnp.where(dz == 0, 0, dz - nz // 2))
        group = ((m + parity) % 2) * n_sub + m // 2
        dx = (ol // 2 - x + 4) % 4
        dcore = (ol % 2 - core + 2) % 2
        return lo, group, half, dx, dcore

    def forward_key(s):
        lo, group, half, dx, dcore = decode(s)
        return jnp.where(dcore == 0, (group * 8 + dx * 2 + half) * LANES + lo, -4096).astype(F32)

    load_s.wait()
    own_slots = slots[0]
    fkey[0] = forward_key(own_slots)

    pl.semaphore_wait(barrier, 3 + nz * ny - 1)

    d2d = [
        remote(slot_hbm, slots.at[1], d2d_send.at[0], d2d_recv.at[0], h, sib),
        remote(g_hbm, g_all.at[1], d2d_send.at[1], d2d_recv.at[1], h, sib),
    ]
    for c in d2d:
        c.start()

    sub_iota = lax.broadcasted_iota(jnp.int32, (LANES, LANES), 0)
    lane_iota = lax.broadcasted_iota(jnp.int32, (LANES, LANES), 1)
    sub_bf = sub_iota.astype(F32).astype(BF16)
    one = jnp.ones((LANES, LANES), BF16)
    zero = jnp.zeros((LANES, LANES), BF16)

    def row_hot(key_row, base):
        rel = jnp.broadcast_to(key_row - base, (LANES, LANES)).astype(BF16)
        return jnp.where(rel == sub_bf, one, zero)

    def slot_sums(group, blocks, cores):
        hot = jnp.concatenate(
            [
                jnp.concatenate(
                    [row_hot(fkey[c, i : i + 1, :], float((group * 8 + b) * LANES)) for c in cores for i in range(nt)], axis=1
                )
                for b in blocks
            ],
            axis=0,
        )
        data = g_all[...].reshape(2 * tokens, feat) if len(cores) == 2 else g_all[cores[0]]
        return jnp.dot(hot, data, preferred_element_type=F32).reshape(len(blocks), plane_rows, feat)

    first_blocks, second_blocks = (4, 5, 3, 6), (2, 7, 0, 1)

    def forward_copy(group, index):
        return remote(
            fsend.at[group, index], frecv.at[group, index], fs_sem.at[group, index], fr_sem.at[group, index],
            h, right if index in (0, 2, 4) else left,
        )

    def compute_first(group):
        if group == 0:
            own = slot_sums(group, first_blocks, (0,))
            for c in d2d:
                c.wait()
            fkey[1] = forward_key(slots[1])
            fsend[group, 0:4] = (own + slot_sums(group, first_blocks, (1,))).astype(BF16)
        else:
            fsend[group, 0:4] = slot_sums(group, first_blocks, (0, 1)).astype(BF16)

    def send_first(group):
        for index in range(4):
            forward_copy(group, index).start()

    def compute_second(group):
        facc[group] = slot_sums(group, second_blocks, (0, 1))

    def merge(group):
        for index, far in ((4, 0), (5, 1)):
            forward_copy(group, far).wait_recv()
            fsend[group, index] = (facc[group, far] + frecv[group, far].astype(F32)).astype(BF16)
            forward_copy(group, index).start()

    def finalize(group):
        m = distance(group)
        for half, (from_left, from_right) in enumerate(((4, 3), (2, 5))):
            plane = 2 * group + half
            forward_copy(group, from_left).wait_recv()
            forward_copy(group, from_right).wait_recv()
            total = facc[group, 2 + half] + frecv[group, from_left].astype(F32) + frecv[group, from_right].astype(F32)
            fin[plane] = total.astype(BF16).reshape(ny, cap, feat)
            to_z = plane_z(group, half)
            back = 2 * m + (half if half == 0 else 1)
            back = jnp.where(m == 0, back, 2 * m + 1 - half)
            for dy in range(ny):
                py = lax.rem(y + dy, ny)
                copy = remote(
                    fin.at[plane, py], grecv.at[back, y], as_sem.at[plane], ar_sem.at[back], to_z * ny + py, l
                )
                if half == 1 and dy == 0:
                    mine = pltpu.make_async_copy(fin.at[plane, y], grecv.at[1, y], ar_sem.at[1])
                    pl.when(m == 0)(mine.start)
                    pl.when(m != 0)(copy.start)
                else:
                    copy.start()

    eye = sub_iota == lane_iota
    span = min(512, rows)

    def column(row):
        return jnp.broadcast_to(row.astype(F32), (LANES, LANES)).T.astype(jnp.int32)

    def column_key(hi, lo):
        return jnp.where(lane_iota == column(lo), column(hi), -1).astype(F32).astype(BF16)

    def rel_plane_z(p):
        m, half = divmod(p, 2)
        dz = nz // 2 - m if half == 0 else ((nz // 2 + m) % nz if m else 0)
        return lax.rem(z + dz, nz)

    one_c = jnp.ones((2 * plane_rows, LANES), BF16)
    zero_c = jnp.zeros((2 * plane_rows, LANES), BF16)

    def planes_of(p, count, src, dst, ssem, rsem):
        return remote(src.at[pl.ds(0, count)], dst.at[pl.ds(0, count)], ssem, rsem, h, sib)

    def owner_step():
        for p in range(nz):
            remote(fin.at[p], grecv.at[p], as_sem.at[p], ar_sem.at[p], h, sib).wait_recv()
        data = grecv[...].reshape(nz * plane_rows, feat)
        keys = [orow[pl.ds(rel_plane_z(p), 1), :] for p in range(nz)]

        def update(i, carry):
            base = (i * span).astype(F32)
            hot = jnp.concatenate(
                [
                    jnp.concatenate([row_hot(key, base + float(j * LANES)) for key in keys], axis=1)
                    for j in range(span // LANES)
                ],
                axis=0,
            )
            grads = jnp.dot(hot, data, preferred_element_type=F32)
            for j in range(span // LANES):
                start = pl.multiple_of(i * span + j * LANES, LANES)
                grad = grads[j * LANES : (j + 1) * LANES]
                mean = jnp.sum(grad * grad, axis=1, keepdims=True) * (1.0 / feat)
                at = i * (span // LANES) + j
                old = jnp.broadcast_to(accum_ref[pl.ds(at, 1), :], (LANES, LANES)).T
                new = old + mean
                acc_v[pl.ds(at, 1), :] = jnp.sum(jnp.where(eye, new, 0.0), axis=0, keepdims=True)
                scale = 0.1 / jnp.sqrt(new)
                scale = jnp.concatenate([scale] * (feat // LANES), axis=1)
                fresh = emb_v[pl.ds(start, LANES), :] - grad * scale
                newemb_v[pl.ds(start, LANES), :] = fresh
                embbf[pl.ds(start, LANES), :] = fresh.astype(BF16)
            return carry

        lax.fori_loop(0, rows // span, update, 0)

        for m in range(n_groups - 1, -1, -1):
            key = []
            for p in (2 * m, 2 * m + 1):
                row = orow[pl.ds(rel_plane_z(p), 1), :]
                hi = jnp.floor(row * (1.0 / LANES))
                key.append(column_key(hi, row - LANES * hi))
            key = jnp.concatenate(key, axis=0)
            hot = jnp.concatenate(
                [jnp.where(key == jnp.asarray(b, BF16), one_c, zero_c) for b in range(rows // LANES)], axis=1
            )
            got = jnp.dot(hot, embbf[...], preferred_element_type=F32).astype(BF16)
            for half in range(2):
                p = 2 * m + half
                pick[p] = got[half * plane_rows : (half + 1) * plane_rows].reshape(ny, cap, feat)
                back = 2 * (parity * n_sub + m // 2) + (half if m == 0 else 1 - half)
                to_z = rel_plane_z(p)
                for dy in range(ny):
                    py = lax.rem(y + dy, ny)
                    if p == 1 and dy == 0:
                        pltpu.make_async_copy(pick.at[p, y], cache.at[0, back, y], rr_sem.at[back]).start()
                    else:
                        remote(
                            pick.at[p, py], cache.at[0, back, y], rs_sem.at[p], rr_sem.at[back], to_z * ny + py, l
                        ).start()

    def gather_copy(group, index):
        pair, first, second = pl.ds(2 * group, 2), 2 * group, 2 * group + 1
        src, dst, to = (
            (cache.at[0, pair], cache.at[6, pair], right),
            (cache.at[0, pair], cache.at[2, pair], left),
            (cache.at[0, pair], cache.at[1, pair], sib),
            (cache.at[6, pair], cache.at[7, pair], sib),
            (cache.at[6, first], cache.at[4, first], right),
            (cache.at[2, pair], cache.at[3, pair], sib),
            (cache.at[2, second], cache.at[4, second], left),
            (cache.at[4, first], cache.at[5, first], sib),
            (cache.at[4, second], cache.at[5, second], sib),
        )[index]
        return remote(src, dst, gs_sem.at[group, index], gr_sem.at[group, index], h, to)

    def own_arrived(group):
        for plane in (2 * group, 2 * group + 1):
            remote(pick.at[0], cache.at[0, plane], rs_sem.at[0], rr_sem.at[plane], h, sib).wait_recv()
        for index in (0, 1, 2):
            gather_copy(group, index).start()

    def near_arrived(group):
        for arrived, onward in ((0, (4, 3)), (1, (6, 5))):
            gather_copy(group, arrived).wait_recv()
            for index in onward:
                gather_copy(group, index).start()

    def far_arrived(group):
        for arrived, onward in ((4, 7), (6, 8)):
            gather_copy(group, arrived).wait_recv()
            gather_copy(group, onward).start()

    tt = min(1024, tokens)
    one_g = jnp.ones((tt, LANES), BF16)
    zero_g = jnp.zeros((tt, LANES), BF16)

    def look_up(chunks, first=False, last=False):
        for lane, group in chunks:
            for index in {1: (2,), 7: (3,), 3: (5,), 5: (7, 8)}.get(lane, ()):
                gather_copy(group, index).wait_recv()

        def step(i, carry):
            at = pl.ds(pl.multiple_of(i * tt, tt), tt)
            key = ekey[at, :]
            blocks = [lane * nz + 2 * group + half for lane, group in chunks for half in range(2)]
            hot = jnp.concatenate([jnp.where(key == jnp.asarray(b, BF16), one_g, zero_g) for b in blocks], axis=1)
            data = jnp.concatenate(
                [cache[lane, pl.ds(2 * group, 2)].reshape(2 * plane_rows, feat) for lane, group in chunks], axis=0
            )
            total = jnp.dot(hot, data, preferred_element_type=F32)
            if not first:
                total += gacc[at, :]
            if last:
                fresh_v[at, :] = total.astype(BF16)
            else:
                gacc[at, :] = total
            return carry

        lax.fori_loop(0, tokens // tt, step, 0)

    def prepare():
        load_o.wait()
        lo, group, half, dx, dcore = decode(own_slots)
        hi = (dx * 2 + dcore) * nz + group * 2 + half
        for i in range(nt):
            ekey[pl.ds(i * LANES, LANES), :] = column_key(hi[i : i + 1, :], lo[i : i + 1, :])
        for i in range(nz):
            orow[i : i + 1, :] = jnp.concatenate(
                [owner_ref[i * ny + k : i * ny + k + 1, :] for k in range(ny)], axis=1
            ).astype(F32)

    def owner_class(value):
        @pl.when(parity == value)
        def _():
            owner_step()

    seen, n_looks = [], sum(op[0] == "L" for op in schedule)
    load_g.wait()
    for op in schedule:
        name, args = op[0], [int(c) for c in op[1:] if op[0] != "L"]
        if name == "C":
            compute_first(*args)
        elif name == "c":
            send_first(*args)
        elif name == "S":
            compute_second(*args)
        elif name == "M":
            merge(*args)
        elif name == "Z":
            finalize(*args)
        elif name == "P":
            prepare()
        elif name == "U":
            if args[0] == 0:
                load_a.wait()
                load_e.wait()
            owner_class(*args)
        elif name == "o":
            own_arrived(*args)
        elif name == "n":
            near_arrived(*args)
        elif name == "f":
            far_arrived(*args)
        elif name == "L":
            seen.append(1)
            look_up([(int(t[0]), int(t[1])) for t in op[1:].split(",")], first=len(seen) == 1, last=len(seen) == n_looks)

    for group in range(n_groups):
        for index in range(6):
            forward_copy(group, index).wait_send()
        for index in range(9):
            gather_copy(group, index).wait_send()
    for p in range(nz):
        group, half = divmod(p, 2)
        whole = remote(fin.at[p], grecv.at[p], as_sem.at[p], ar_sem.at[p], h, sib)
        if half == 0 or group % n_sub:
            whole.wait_send()
        else:
            part = remote(
                fin.at[p, pl.ds(0, ny - 1)], grecv.at[p, pl.ds(0, ny - 1)], as_sem.at[p], ar_sem.at[p], h, sib
            )
            m = distance(group)
            pl.when(m == 0)(part.wait_send)
            pl.when(m != 0)(whole.wait_send)
        count = ny - 1 if p == 1 else ny
        remote(
            pick.at[p, pl.ds(0, count)], cache.at[0, p, pl.ds(0, count)], rs_sem.at[p], rr_sem.at[p], h, sib
        ).wait_send()


def hand_over(emb_in, acc_in, fresh_in, emb_out, acc_out, fresh_out, sem):
    copies = []
    for src, dst, pieces in ((emb_in, emb_out, 4), (fresh_in, fresh_out, 2), (acc_in, acc_out, 1)):
        size = src.shape[0] // pieces
        for i in range(pieces):
            part = pl.ds(i * size, size)
            copies.append(pltpu.make_async_copy(src.at[part], dst.at[part], sem.at[len(copies)]))
    for c in copies:
        c.start()
    for c in copies:
        c.wait()


def local(ny, embedding, row_accum, lookup_grads, lookup_slot, owner_rows):
    n_hst = lax.axis_size("hst")
    nz = n_hst // ny
    rows, feat = embedding.shape
    tokens = lookup_slot.shape[0]
    cap = owner_rows.shape[2]
    nt = tokens // LANES
    groups = nz // 2
    plane = ny * cap
    vmem = pl.BlockSpec(memory_space=pltpu.VMEM)
    hbm = pl.BlockSpec(memory_space=pltpu.HBM)
    dma = pltpu.SemaphoreType.DMA
    outs = (
        jax.ShapeDtypeStruct((rows, feat), F32),
        jax.ShapeDtypeStruct((rows // LANES, LANES), F32),
        jax.ShapeDtypeStruct((tokens, feat), BF16),
    )
    results = pl.pallas_call(
        functools.partial(kernel, SCHEDULES[groups], nz, ny, cap),
        out_shape=tuple(pltpu.VMEM(o.shape, o.dtype) for o in outs),
        in_specs=[hbm] * 5,
        out_specs=(vmem, vmem, vmem),
        scratch_shapes=[
            pltpu.VMEM((2, nt, LANES), jnp.int32),
            pltpu.VMEM((n_hst, cap), jnp.int32),
            pltpu.VMEM((rows // LANES, LANES), F32),
            pltpu.VMEM((2, tokens, feat), BF16),
            pltpu.VMEM((2, nt, LANES), F32),
            pltpu.VMEM((nz, LANES), F32),
            pltpu.VMEM((groups, 4, plane, feat), F32),
            pltpu.VMEM((groups, 6, plane, feat), BF16),
            pltpu.VMEM((groups, 6, plane, feat), BF16),
            pltpu.VMEM((nz, ny, cap, feat), BF16),
            pltpu.VMEM((nz, ny, cap, feat), BF16),
            pltpu.VMEM((rows, feat), F32),
            pltpu.VMEM((rows, feat), BF16),
            pltpu.VMEM((nz, ny, cap, feat), BF16),
            pltpu.VMEM((8, nz, ny, cap, feat), BF16),
            pltpu.VMEM((tokens, LANES), BF16),
            pltpu.VMEM((tokens, feat), F32),
            dma((5,)),
            dma((2,)),
            dma((2,)),
            dma((groups, 6)),
            dma((groups, 6)),
            dma((nz,)),
            dma((nz,)),
            dma((nz,)),
            dma((nz,)),
            dma((groups, 9)),
            dma((groups, 9)),
        ],
        compiler_params=pltpu.CompilerParams(
            collective_id=0, has_side_effects=True, vmem_limit_bytes=44 * 1024 * 1024
        ),
    )(
        *(
            pltpu.with_memory_space_constraint(a, pltpu.HBM)
            for a in (
                lookup_slot.reshape(nt, LANES),
                lookup_grads,
                owner_rows.reshape(n_hst, cap),
                row_accum.reshape(rows // LANES, LANES),
                embedding,
            )
        )
    )
    new_embedding, new_accum, fresh = pl.pallas_call(
        hand_over,
        out_shape=outs,
        in_specs=[vmem, vmem, vmem],
        out_specs=(hbm, hbm, hbm),
        scratch_shapes=[dma((7,))],
    )(*(pltpu.with_memory_space_constraint(r, pltpu.VMEM) for r in results))
    return new_embedding, new_accum.reshape(rows), fresh


def solution(mesh, ny=NY):
    both = ("hst", "local")
    return jax.shard_map(
        functools.partial(local, ny),
        mesh=mesh,
        in_specs=(P(both, None), P(both), P(both, None), P(both), P(both, None, None)),
        out_specs=(P(both, None), P(both), P(both, None)),
        check_vma=False,
    )
```

time: 311 us -> 79.8 us (0.26)
  blocking collectives: 129 us -> 0 us
  waiting for transfers between devices: 109 us -> 0 us
  Pallas kernels: 0 us -> 78.3 us
  local copies, waits for them, and re-layouts: 25.2 us -> 0 us
  matrix products: 20.3 us -> 0 us
  between operations: 14.2 us -> 0.8 us
  other arithmetic: 12.4 us -> 0 us
    all_to_all x2 -> x0, blocking collectives: 129 us -> none  [the longest x1 106 us: local(): lax.all_to_all(partial_value, 'hst', split_axis=0, concat_axis=0, tiled=T...]
    pallas_call x0 -> x2, Pallas kernels: none -> 78.3 us  [the longest x1 76.6 us: local(): pl.pallas_call(functools.partial(kernel, SCHEDULES[groups], nz, ny, cap),...]
    unnamed x3 -> x0, waiting for transfers between devices: 74 us -> none
    all_gather x1 -> x0, waiting for transfers between devices: 34.7 us -> none  [local(): lax.all_gather(returned, 'local', axis=1, tiled=True)]
    dot_general x1 -> x0, matrix products: 20.3 us -> none  [local(): lax.dot_general(onehot, lookup_grads, (((0,), (0,)), ((), ())), preferred...]
    gather x2 -> x0, local copies, waits for them, and re-layouts: 14 us -> none  [the longest x1 9.36 us: local(): fresh_rows = jnp.take(host_cache, lookup_slot, axis=0)]
    scatter-add x1 -> x0, other arithmetic: 6.86 us -> none  [local(): jax.ops.segment_sum(received.reshape(n_hst * capacity, feat_width), targe...]
    unnamed x18 -> x0, local copies, waits for them, and re-layouts: 6.32 us -> none
  transfers between devices with their start and end apart: 2 -> 0, of which waited for: 2 -> 0; matrix products, arithmetic and copies ran while one was open for 0% -> 0% of each run, Pallas kernels for 0% -> 0%
where the time goes in v2:
time: 79.8 us; the launch traced here: 79.1 us
  Pallas kernels  78.3 us (98%)
  between operations  0.8 us (1%)
    pallas_call x1, Pallas kernels, local(): pl.pallas_call(functools.partial(kernel, SCHEDULES[groups], nz, ny, cap),...  76.6 us
    pallas_call x1, Pallas kernels, local(): pl.pallas_call(hand_over, out_shape=outs, in_specs=[vmem, vmem, vmem], ou...  1.72 us

profile of v2, /device:TPU:1, one launch (start us, length us, event | category | flops | bytes accessed | tf_op | source)
XLA Modules:
  0.0 79.1 jit_solution(5770049093045414741)
XLA Ops:
  0.6 76.6 %shard_map.76 = (f32[2048,256]{1,0:T(8,128)S(1)}, f32[16,128]{1,0:T(8,128)S(1)}, bf16[2048,256]{1,0:T(8,128)(2,1)S(1)}) custom-call(s32[16,128]{1,0:T(8,128)} %bitcast.5, bf16[2048,256]{1,0:T(8,128)(2,1)} %g_hbm.1, s32[32,32]{1,0:T(8,128)} %bitcast.4, f32[16,128]{1,0:T(8,128)} %bitcast.6, f32[2048,256]{1,0:T(8,128)} %emb_hbm.1), custom_call_target="tpu_custom_call" | custom-call | tf_op jit(solution)/shard_map/pallas_call | solution.py:440
  77.3 1.7 %shard_map.77 = (f32[2048,256]{1,0:T(8,128)}, f32[16,128]{1,0:T(8,128)}, bf16[2048,256]{1,0:T(8,128)(2,1)}) custom-call(f32[2048,256]{1,0:T(8,128)S(1)} %get-tuple-element.9.emb_in, f32[16,128]{1,0:T(8,128)S(1)} %get-tuple-element.10.acc_in, bf16[2048,256]{1,0:T(8,128)(2,1)S(1)} %get-tuple-element.11.fresh_in), custom_call_target="tpu_custom_call" | custom-call | tf_op jit(solution)/shard_map/pallas_call | solution.py:490

commit v3 on v2

--- a/solution.py
+++ b/solution.py
@@ -226,7 +226,7 @@
         keys = [orow[pl.ds(rel_plane_z(p), 1), :] for p in range(nz)]
 
         def update(i, carry):
-            base = (i * span).astype(F32)
+            base = jnp.asarray(i * span, F32)
             hot = jnp.concatenate(
                 [
                     jnp.concatenate([row_hot(key, base + float(j * LANES)) for key in keys], axis=1)
@@ -250,7 +250,7 @@
                 embbf[pl.ds(start, LANES), :] = fresh.astype(BF16)
             return carry
 
-        lax.fori_loop(0, rows // span, update, 0)
+        lax.fori_loop(0, rows // span, update, 0, unroll=True)
 
         for m in range(n_groups - 1, -1, -1):
             key = []
@@ -280,8 +280,8 @@
     def gather_copy(group, index):
         pair, first, second = pl.ds(2 * group, 2), 2 * group, 2 * group + 1
         src, dst, to = (
-            (cache.at[0, pair], cache.at[6, pair], right),
-            (cache.at[0, pair], cache.at[2, pair], left),
+            (cache.at[0, first], cache.at[6, first], right),
+            (cache.at[0, second], cache.at[2, second], left),
             (cache.at[0, pair], cache.at[1, pair], sib),
             (cache.at[6, pair], cache.at[7, pair], sib),
             (cache.at[6, first], cache.at[4, first], right),
@@ -289,20 +289,21 @@
             (cache.at[2, second], cache.at[4, second], left),
             (cache.at[4, first], cache.at[5, first], sib),
             (cache.at[4, second], cache.at[5, second], sib),
+            (cache.at[0, second], cache.at[6, second], right),
+            (cache.at[0, first], cache.at[2, first], left),
         )[index]
         return remote(src, dst, gs_sem.at[group, index], gr_sem.at[group, index], h, to)
 
     def own_arrived(group):
         for plane in (2 * group, 2 * group + 1):
             remote(pick.at[0], cache.at[0, plane], rs_sem.at[0], rr_sem.at[plane], h, sib).wait_recv()
-        for index in (0, 1, 2):
+        for index in (0, 1, 9, 10, 2):
             gather_copy(group, index).start()
 
     def near_arrived(group):
-        for arrived, onward in ((0, (4, 3)), (1, (6, 5))):
+        for arrived, onward in ((0, 4), (1, 6), (9, 3), (10, 5)):
             gather_copy(group, arrived).wait_recv()
-            for index in onward:
-                gather_copy(group, index).start()
+            gather_copy(group, onward).start()
 
     def far_arrived(group):
         for arrived, onward in ((4, 7), (6, 8)):
@@ -335,7 +336,7 @@
                 gacc[at, :] = total
             return carry
 
-        lax.fori_loop(0, tokens // tt, step, 0)
+        lax.fori_loop(0, tokens // tt, step, 0, unroll=True)
 
     def prepare():
         load_o.wait()
@@ -387,7 +388,7 @@
     for group in range(n_groups):
         for index in range(6):
             forward_copy(group, index).wait_send()
-        for index in range(9):
+        for index in range(11):
             gather_copy(group, index).wait_send()
     for p in range(nz):
         group, half = divmod(p, 2)
@@ -469,8 +470,8 @@
             dma((nz,)),
             dma((nz,)),
             dma((nz,)),
-            dma((groups, 9)),
-            dma((groups, 9)),
+            dma((groups, 11)),
+            dma((groups, 11)),
         ],
         compiler_params=pltpu.CompilerParams(
             collective_id=0, has_side_effects=True, vmem_limit_bytes=44 * 1024 * 1024

time: 79.8 us -> 76.9 us (0.964)
  Pallas kernels: 78.3 us -> 75.9 us
    pallas_call x1, Pallas kernels: 76.6 us -> 74.2 us  [local(): pl.pallas_call(functools.partial(kernel, SCHEDULES[groups], nz, ny, cap),...]
where the time goes in v3:
time: 76.9 us; the launch traced here: 76.7 us
  Pallas kernels  75.9 us (99%)
  between operations  0.8 us (1%)
    pallas_call x1, Pallas kernels, local(): pl.pallas_call(functools.partial(kernel, SCHEDULES[groups], nz, ny, cap),...  74.2 us
    pallas_call x1, Pallas kernels, local(): pl.pallas_call(hand_over, out_shape=outs, in_specs=[vmem, vmem, vmem], ou...  1.72 us

profile of v3, /device:TPU:1, one launch (start us, length us, event | category | flops | bytes accessed | tf_op | source)
XLA Modules:
  0.0 76.7 jit_solution(11901959395737813245)
XLA Ops:
  0.6 74.2 %shard_map.76 = (f32[2048,256]{1,0:T(8,128)S(1)}, f32[16,128]{1,0:T(8,128)S(1)}, bf16[2048,256]{1,0:T(8,128)(2,1)S(1)}) custom-call(s32[16,128]{1,0:T(8,128)} %bitcast.5, bf16[2048,256]{1,0:T(8,128)(2,1)} %g_hbm.1, s32[32,32]{1,0:T(8,128)} %bitcast.4, f32[16,128]{1,0:T(8,128)} %bitcast.6, f32[2048,256]{1,0:T(8,128)} %emb_hbm.1), custom_call_target="tpu_custom_call" | custom-call | tf_op jit(solution)/shard_map/pallas_call | solution.py:441
  74.8 1.7 %shard_map.77 = (f32[2048,256]{1,0:T(8,128)}, f32[16,128]{1,0:T(8,128)}, bf16[2048,256]{1,0:T(8,128)(2,1)}) custom-call(f32[2048,256]{1,0:T(8,128)S(1)} %get-tuple-element.9.emb_in, f32[16,128]{1,0:T(8,128)S(1)} %get-tuple-element.10.acc_in, bf16[2048,256]{1,0:T(8,128)(2,1)S(1)} %get-tuple-element.11.fresh_in), custom_call_target="tpu_custom_call" | custom-call | tf_op jit(solution)/shard_map/pallas_call | solution.py:491

commit v4 on v3

--- a/solution.py
+++ b/solution.py
@@ -14,7 +14,7 @@
 LANES = 128
 SCHEDULES = {
     4: (
-        "C0", "c0", "S0", "C1", "c1", "S1", "M0", "C2", "M1", "c2", "S2", "C3", "c3", "Z0", "P", "Z1", "S3", "M2", "M3",
+        "C0", "c0", "S0", "C1", "c1", "S1", "M0", "C2", "M1", "c2", "S2", "C3", "c3", "Z0", "Z1", "S3", "M2", "M3", "P",
         "Z2", "Z3", "U0", "U1", "o1", "o0", "n1", "n0", "o3", "o2", "L00,01,10,11", "f1", "f0", "L61,21,71,31", "n3",
         "n2", "L60,20,70,30", "f3", "L40,41,50,51", "L02,03,12,13", "f2", "L63,23,73,33", "L62,22,72,32,43,53", "L42,52",
     ),
@@ -220,23 +220,33 @@
         return remote(src.at[pl.ds(0, count)], dst.at[pl.ds(0, count)], ssem, rsem, h, sib)
 
     def owner_step():
-        for p in range(nz):
-            remote(fin.at[p], grecv.at[p], as_sem.at[p], ar_sem.at[p], h, sib).wait_recv()
-        data = grecv[...].reshape(nz * plane_rows, feat)
         keys = [orow[pl.ds(rel_plane_z(p), 1), :] for p in range(nz)]
 
-        def update(i, carry):
-            base = jnp.asarray(i * span, F32)
+        def sums(i, planes):
             hot = jnp.concatenate(
                 [
-                    jnp.concatenate([row_hot(key, base + float(j * LANES)) for key in keys], axis=1)
+                    jnp.concatenate([row_hot(keys[p], float(i * span + j * LANES)) for p in planes], axis=1)
                     for j in range(span // LANES)
                 ],
                 axis=0,
             )
-            grads = jnp.dot(hot, data, preferred_element_type=F32)
+            data = grecv[planes[0] : planes[-1] + 1].reshape(len(planes) * plane_rows, feat)
+            return jnp.dot(hot, data, preferred_element_type=F32)
+
+        def arrived(planes):
+            for p in planes:
+                remote(fin.at[p], grecv.at[p], as_sem.at[p], ar_sem.at[p], h, sib).wait_recv()
+
+        early, late = range(nz // 2), range(nz // 2, nz)
+        arrived(early)
+        for i in range(rows // span):
+            gacc[pl.ds(i * span, span), :] = sums(i, early)
+        arrived(late)
+
+        def update(i):
+            grads = gacc[pl.ds(i * span, span), :] + sums(i, late)
             for j in range(span // LANES):
-                start = pl.multiple_of(i * span + j * LANES, LANES)
+                start = i * span + j * LANES
                 grad = grads[j * LANES : (j + 1) * LANES]
                 mean = jnp.sum(grad * grad, axis=1, keepdims=True) * (1.0 / feat)
                 at = i * (span // LANES) + j
@@ -248,9 +258,9 @@
                 fresh = emb_v[pl.ds(start, LANES), :] - grad * scale
                 newemb_v[pl.ds(start, LANES), :] = fresh
                 embbf[pl.ds(start, LANES), :] = fresh.astype(BF16)
-            return carry
-
-        lax.fori_loop(0, rows // span, update, 0, unroll=True)
+
+        for i in range(rows // span):
+            update(i)
 
         for m in range(n_groups - 1, -1, -1):
             key = []

time: 76.9 us -> 76.2 us (level)
  Pallas kernels: 75.9 us -> 74.9 us
    pallas_call x1, Pallas kernels: 74.2 us -> 73.2 us  [local(): pl.pallas_call(functools.partial(kernel, SCHEDULES[groups], nz, ny, cap),...]
where the time goes in v4:
time: 76.2 us; the launch traced here: 75.7 us
  Pallas kernels  74.9 us (98%)
  between operations  0.8 us (1%)
    pallas_call x1, Pallas kernels, local(): pl.pallas_call(functools.partial(kernel, SCHEDULES[groups], nz, ny, cap),...  73.2 us
    pallas_call x1, Pallas kernels, local(): pl.pallas_call(hand_over, out_shape=outs, in_specs=[vmem, vmem, vmem], ou...  1.72 us

profile of v4, /device:TPU:1, one launch (start us, length us, event | category | flops | bytes accessed | tf_op | source)
XLA Modules:
  0.0 75.7 jit_solution(10989084480585050623)
XLA Ops:
  0.6 73.2 %shard_map.76 = (f32[2048,256]{1,0:T(8,128)S(1)}, f32[16,128]{1,0:T(8,128)S(1)}, bf16[2048,256]{1,0:T(8,128)(2,1)S(1)}) custom-call(s32[16,128]{1,0:T(8,128)} %bitcast.5, bf16[2048,256]{1,0:T(8,128)(2,1)} %g_hbm.1, s32[32,32]{1,0:T(8,128)} %bitcast.4, f32[16,128]{1,0:T(8,128)} %bitcast.6, f32[2048,256]{1,0:T(8,128)} %emb_hbm.1), custom_call_target="tpu_custom_call" | custom-call | tf_op jit(solution)/shard_map/pallas_call | solution.py:451
  73.8 1.7 %shard_map.77 = (f32[2048,256]{1,0:T(8,128)}, f32[16,128]{1,0:T(8,128)}, bf16[2048,256]{1,0:T(8,128)(2,1)}) custom-call(f32[2048,256]{1,0:T(8,128)S(1)} %get-tuple-element.9.emb_in, f32[16,128]{1,0:T(8,128)S(1)} %get-tuple-element.10.acc_in, bf16[2048,256]{1,0:T(8,128)(2,1)S(1)} %get-tuple-element.11.fresh_in), custom_call_target="tpu_custom_call" | custom-call | tf_op jit(solution)/shard_map/pallas_call | solution.py:501
